TPU v7x, 256 devices: a whole 4x4x8 slice. The times are simulated.
256 devices in a mesh: tm: 64 (over z, y, core), tp: 4 (over x).
Axes of the slice: x: 4, y: 4, z: 8, core: 2. Of those that a mesh axis runs over, the one named last changes fastest.
Arguments:
- starts: float32 [64, 128, 3072], P('tm', None, 'tp'), may hold values from -6 to 6
- modulation: float32 [64, 3, 3072], P('tm'), may hold values from -5 to 5
- w_qkv: bfloat16 [3072, 3, 1536], P(None, None, 'tp'), may hold values from -0.109375 to 0.109375
- norm_gain: float32 [2, 128], replicated, may hold values from 1.5 to 8
- w_out: bfloat16 [1536, 3072], P('tp'), may hold values from -0.15625 to 0.15625
- offset: int32 [1], replicated, may hold values from 0 to 128
Outputs:
- updated: float32 [64, 128, 3072], P('tm', None, 'tp')
- drift: float32 [64, 128, 3072], P('tm', None, 'tp')
- residual: float32 [64], P('tm')
All inputs are finite; a program needn't handle non-finite values.
Results may differ from a plain program's by a relative error of at most 0.0018.
The roundings to bfloat16 on the way count: a program that leaves them out, or rounds other values in their place, can miss the bound.
Values may be sent and summed in bfloat16 or wider, within the bound.
A program may use at most 128 MiB of HBM per device.

v0:
```python
import jax
import jax.numpy as jnp
from jax import lax
from jax.sharding import PartitionSpec as P

HEAD = 128


EPSILON = 1e-06


def entering(part, axis, combine, identity):
    place = lax.axis_index(axis)
    gathered = lax.all_gather(part, axis)
    state = jnp.zeros_like(part) + jnp.asarray(identity, part.dtype)

    def one(step, state):
        return combine(state, lax.dynamic_index_in_dim(gathered, step, 0, False))

    return lax.fori_loop(0, place, one, state)


def noise_level(position, total_steps):
    fraction = 1.0 - position / total_steps
    return 3.0 * fraction / (1.0 + 2.0 * fraction)


def rms_scale(tensor, gain):
    return tensor * lax.rsqrt(jnp.mean(tensor * tensor, axis=-1, keepdims=True) + EPSILON) * gain


def add_terms(earlier, later):
    return earlier + later


def body(starts, modulation, w_qkv, norm_gain, w_out, offset):
    latent = starts[0]
    tokens = latent.shape[0]
    columns = latent.shape[1]
    model_width = w_out.shape[1]
    heads_here = w_out.shape[0] // HEAD
    column_block = lax.axis_index("tp")
    time_index = lax.axis_index("tm")
    modulate = modulation[0]
    own_modulate = lax.dynamic_slice_in_dim(modulate, column_block * columns, columns, 1)
    gathered = lax.all_gather(latent, "tp", axis=1, tiled=True)
    row_mean = jnp.mean(gathered, axis=1, keepdims=True)
    centered = gathered - row_mean
    row_var = jnp.mean(centered * centered, axis=1, keepdims=True)
    normed = centered * lax.rsqrt(row_var + EPSILON)
    modin = (normed * (1.0 + modulate[1]) + modulate[0]).astype(jnp.bfloat16)
    joined = w_qkv.reshape(model_width, 3 * heads_here * HEAD)
    projected = jnp.dot(modin, joined, preferred_element_type=jnp.float32).reshape(
        tokens, 3, heads_here, HEAD
    )
    queries = rms_scale(projected[:, 0], norm_gain[0])
    keys_here = rms_scale(projected[:, 1], norm_gain[1])
    scores = jnp.einsum(
        "qhe,khe->hqk", queries, keys_here, precision=lax.Precision.HIGHEST
    ) / jnp.sqrt(jnp.float32(HEAD))
    probs = jax.nn.softmax(scores, axis=-1).astype(jnp.bfloat16)
    values_bf = projected[:, 2].astype(jnp.bfloat16)
    heads = jnp.einsum("hqk,khe->qhe", probs, values_bf, preferred_element_type=jnp.float32)
    heads = heads.astype(jnp.bfloat16).reshape(tokens, heads_here * HEAD)
    partial_out = jnp.dot(heads, w_out, preferred_element_type=jnp.float32)
    summed = lax.psum(partial_out, "tp")
    attended = lax.dynamic_slice_in_dim(summed, column_block * columns, columns, 1)
    drift = latent + own_modulate[2] * attended
    total_steps = jnp.float32(lax.axis_size("tm") * 3)
    position = (offset[0] + time_index).astype(jnp.float32)
    step_size = noise_level(position + 1.0, total_steps) - noise_level(position, total_steps)
    is_first = time_index == 0
    anchor_part = jnp.where(is_first, latent, jnp.zeros_like(latent))
    contribution = step_size * drift + anchor_part
    earlier_sum = entering(contribution, "tm", add_terms, jnp.zeros_like(contribution))
    fresh = earlier_sum + anchor_part
    new_end = earlier_sum + contribution
    change = fresh - latent
    squared = lax.psum(jnp.sum(change * change), "tp")
    residual_value = squared / (tokens * model_width)
    return (new_end[None], drift[None], residual_value.reshape(1))


def solution(mesh):
    in_specs = (
        P("tm", None, "tp"),
        P("tm", None, None),
        P(None, None, "tp"),
        P(),
        P("tp", None),
        P(),
    )
    out_specs = (P("tm", None, "tp"), P("tm", None, "tp"), P("tm"))
    return jax.shard_map(body, mesh=mesh, in_specs=in_specs, out_specs=out_specs, check_vma=False)
```

profile of v0, /device:TPU:248, one launch (start us, length us, event | category | flops | bytes accessed | tf_op | source)
XLA Modules:
  0.0 316.4 jit_solution(6107864125589516688)
XLA Ops:
  8.0 10.3 %copy.12 = bf16[3072,3,384]{0,2,1:T(8,128)(2,1)} copy(bf16[3072,3,384]{2,0,1:T(8,128)(2,1)} %param.10) | data formatting | bytes 14155776 | tf_op args[2]
  18.3 20.8 %all-gather.5.cloned.1.call-done = f32[1,128,3072]{2,1,0:T(8,128)} async-done(((f32[1,128,768]{2,1,0:T(8,128)}), f32[1,128,3072]{2,1,0:T(8,128)}) %all-gather.5.cloned.1.call-update) | async-done | bytes 1572880 | tf_op jit(solution)/shard_map/all_gather | solution.py:46
  39.1 1.6 reduce_sum.54
  40.6 1.8 multiply_reduce_fusion
  42.5 5.1 %fusion.4 = f32[128,3,3,128]{0,3,2,1:T(8,128)S(1)} fusion(bf16[3,3,128,3072]{3,2,1,0:T(8,128)(2,1)} %bitcast.78, f32[1,128,3072]{2,1,0:T(8,128)S(1)} %copy-done.1, f32[3072]{0:T(1024)S(1)} %bitcast.82, f32[3072]{0:T(1024)S(1)} %bitcast.81, f32[128]{0:T(128)S(1)} %add_rsqrt_fusion.2, f32[128]{0:T(128)S(1)} %broadcast_multiply_fusion), kind=kOutput, calls=%fused_computation.10 | convolution fusion | flops 907935744 | bytes 9266176 | tf_op jit(solution)/shard_map/dot_general | solution.py:53
  48.6 1.8 fusion.26
  51.3 54.9 %all-reduce.2.cloned.1.call-done = f32[128,3072]{1,0:T(8,128)} async-done(((f32[128,3072]{1,0:T(8,128)}), f32[128,3072]{1,0:T(8,128)}) %all-reduce.2.cloned.1.call-update) | async-done | bytes 1572880 | tf_op jit(solution)/shard_map/psum | solution.py:66
  106.2 1.9 fusion.16
  108.2 119.0 %all-gather.7.cloned.1.call-done = f32[8192,768]{1,0:T(8,128)} async-done(((f32[128,768]{1,0:T(8,128)}), f32[8192,768]{1,0:T(8,128)}) %all-gather.7.cloned.1.call-update) | async-done | bytes 25165840 | tf_op jit(solution)/shard_map/all_gather | solution.py:14
  227.2 68.4 %while.10 = (s32[]{:T(128)}, f32[128,768]{1,0:T(8,128)S(1)}, s32[]{:T(128)}, f32[64,128,768]{2,1,0:T(8,128)}, s32[]{:T(128)}, /*index=5*/s32[]{:T(128)}, s32[]{:T(128)}) while((s32[]{:T(128)}, f32[128,768]{1,0:T(8,128)S(1)}, s32[]{:T(128)}, f32[64,128,768]{2,1,0:T(8,128)}, s32[]{:T(128)}, /*index=5*/s32[]{:T(128)}, s32[]{:T(128)}) %tuple.37), condition=%wide.region_8.9_spmd, body=%wide.region_7.8_spmd.sunk | while | flops 98309 | bytes 1179771 | solution.py:20
  227.2 1.1 bitcast_add_fusion.3
  228.4 1.1 bitcast_add_fusion.3
  229.5 1.1 bitcast_add_fusion.3
  230.6 1.1 bitcast_add_fusion.3
  231.7 1.1 bitcast_add_fusion.3
  232.8 1.1 bitcast_add_fusion.3
  233.9 1.1 bitcast_add_fusion.3
  235.0 1.1 bitcast_add_fusion.3
  236.1 1.1 bitcast_add_fusion.3
  237.2 1.1 bitcast_add_fusion.3
  238.3 1.1 bitcast_add_fusion.3
  239.4 1.1 bitcast_add_fusion.3
  240.5 1.1 bitcast_add_fusion.3
  241.6 1.1 bitcast_add_fusion.3
  242.7 1.1 bitcast_add_fusion.3
  243.8 1.1 bitcast_add_fusion.3
  244.9 1.1 bitcast_add_fusion.3
  246.0 1.1 bitcast_add_fusion.3
  247.1 1.1 bitcast_add_fusion.3
  248.2 1.1 bitcast_add_fusion.3
  249.3 1.1 bitcast_add_fusion.3
  250.4 1.1 bitcast_add_fusion.3
  251.5 1.1 bitcast_add_fusion.3
  252.6 1.1 bitcast_add_fusion.3
  253.7 1.1 bitcast_add_fusion.3
  254.8 1.1 bitcast_add_fusion.3
  255.9 1.1 bitcast_add_fusion.3
  257.0 1.1 bitcast_add_fusion.3
  258.1 1.1 bitcast_add_fusion.3
  259.2 1.1 bitcast_add_fusion.3
  260.4 1.1 bitcast_add_fusion.3
  261.5 1.1 bitcast_add_fusion.3
  262.6 1.1 bitcast_add_fusion.3
  263.7 1.1 bitcast_add_fusion.3
  264.8 1.1 bitcast_add_fusion.3
  265.9 1.1 bitcast_add_fusion.3
  295.6 1.4 fusion.11
  297.0 11.0 %psum.15 = f32[]{:T(128)} all-reduce(f32[]{:T(128)} %get-tuple-element.39), channel_id=1, replica_groups=mesh['tm'=64,'tp'=4] {'tp'}, use_global_device_ids=true, to_apply=%region_10.11 | all-reduce | flops 1 | bytes 8 | tf_op jit(solution)/shard_map/psum | solution.py:79
  (55 shorter events, 30.0 us)
Async XLA Ops:
  7.2 41.4 %copy-start = (bf16[384,3072]{1,0:T(8,128)(2,1)S(1)}, bf16[384,3072]{1,0:T(8,128)(2,1)}, u32[]{:S(2)}) copy-start(bf16[384,3072]{1,0:T(8,128)(2,1)} %param.12) | copy-start | bytes 7077892
  7.2 31.9 %all-gather.5.cloned.1.call-start = ((), (), s32[]{:S(2)}) async-start(), calls=%async_computation.1 | async-start | bytes 1966080 | tf_op jit(solution)/shard_map/all_gather | solution.py:46
  7.9 10.4 %copy-start.5 = (f32[2,128]{1,0:T(2,128)S(1)}, f32[2,128]{1,0:T(2,128)}, u32[]{:S(2)}) copy-start(f32[2,128]{1,0:T(2,128)} %param.11) | copy-start | bytes 3076
  7.9 10.3 %copy-start.4 = (f32[1,3,3072]{2,0,1:T(1,128)S(1)}, f32[1,3,3072]{2,0,1:T(1,128)}, u32[]{:S(2)}) copy-start(f32[1,3,3072]{2,0,1:T(1,128)} %param.9) | copy-start | bytes 110596
  7.9 98.3 %all-reduce.2.cloned.1.call-start = ((), (), s32[]{:S(2)}) async-start(), calls=%async_computation | async-start | bytes 3145728 | tf_op jit(solution)/shard_map/psum | solution.py:66
  40.6 1.9 copy-start.1
  50.4 55.8 %copy-start.2 = (f32[1,128,768]{2,1,0:T(8,128)S(1)}, f32[1,128,768]{2,1,0:T(8,128)}, u32[]{:S(2)}) copy-start(f32[1,128,768]{2,1,0:T(8,128)} %param.8) | copy-start | bytes 1179652
  50.4 176.8 %all-gather.7.cloned.1.call-start = ((), (), s32[]{:S(2)}) async-start(), calls=%async_computation.2 | async-start | bytes 25559040 | tf_op jit(solution)/shard_map/all_gather | solution.py:14
  227.2 68.4 %copy-start.3 = (f32[128,768]{1,0:T(8,128)S(1)}, f32[128,768]{1,0:T(8,128)}, u32[]{:S(2)}) copy-start(f32[128,768]{1,0:T(8,128)} %get-tuple-element.38) | copy-start | bytes 1179652
Sparse Core Ops, SparseCore 0:
  9.8 29.1 all-gather.4
  50.5 55.6 all-reduce.1
  109.5 117.5 all-gather.6
where the time goes:
time: 319 us; the launch traced here: 316 us
  waiting for transfers between devices  195 us (61%)
  other arithmetic  73.9 us (23%)
  between operations  16.4 us (5%)
  blocking collectives  11 us (3%)
  local copies, waits for them, and re-layouts  10.4 us (3%)
  matrix products  7.68 us (2%)
    all_gather x1, waiting for transfers between devices, entering(): gathered = lax.all_gather(part, axis)  119 us
    add x62, other arithmetic, add_terms(): return earlier + later  67 us
    psum x1, waiting for transfers between devices, body(): summed = lax.psum(partial_out, 'tp')  54.9 us
    all_gather x1, waiting for transfers between devices, body(): gathered = lax.all_gather(latent, 'tp', axis=1, tiled=True)  20.8 us
    psum x1, blocking collectives, body(): squared = lax.psum(jnp.sum(change * change), 'tp')  11 us
    unnamed x13, local copies, waits for them, and re-layouts  10.3 us
  transfers between devices with their start and end apart: 3, of which 3 were waited for; matrix products, arithmetic and copies ran while one was open for 3% of the time, Pallas kernels for 0%

commit v1 on v0

v1 whole, which is shorter than its diff:
```python
import functools

import jax
import jax.numpy as jnp
from jax import lax
from jax.experimental import pallas as pl
from jax.experimental.pallas import tpu as pltpu
from jax.sharding import PartitionSpec as P

HEAD = 128
EPSILON = 1e-06
MESH = pl.DeviceIdType.MESH

NX = 4
NQ = 8
NZ = 8
PARTS = 2


class Copies:
    def __init__(self, send, recv):
        self.send, self.recv, self.used = send, recv, 0

    def remote(self, src, dst, device):
        at = self.used
        self.used += 1
        return pltpu.make_async_remote_copy(
            src_ref=src,
            dst_ref=dst,
            send_sem=self.send.at[at],
            recv_sem=self.recv.at[at],
            device_id=device,
            device_id_type=MESH,
        )


REMOTE = 3 + 3 + 7 + 7 + 7 + PARTS * (3 + 7 + 7 + 7) + 3


def kernel(
    starts_hbm, mod_hbm, wq_hbm, gain_ref, wo_hbm, off_ref,
    upd_hbm, drift_hbm, res_ref,
    lat, mod, wq, wo, st, xin, acc, heads, psend, precv, s0p, s0,
    csend, arecv, bsend, brecv, csum, esend, erecv, cown, drift, upd, rs,
    local_sem, send_sem, recv_sem,
):
    tokens, cols = lat.shape
    half = cols // PARTS
    rows = tokens // NQ
    tm = lax.axis_index("tm")
    x = lax.axis_index("tp")
    z = tm // NQ
    q = tm % NQ
    cp = Copies(send_sem, recv_sem)

    def xpeer(d):
        return (tm, lax.rem(x + d, NX))

    def qpeer(r):
        return (z * NQ + lax.rem(q + r, NQ), x)

    def zpeer(r):
        return (lax.rem(z + r, NZ) * NQ + q, x)

    barrier = pltpu.get_barrier_semaphore()
    for d in range(1, NX):
        pl.semaphore_signal(barrier, inc=1, device_id=xpeer(d), device_id_type=MESH)
    for r in range(1, NQ):
        pl.semaphore_signal(barrier, inc=1, device_id=qpeer(r), device_id_type=MESH)
    for r in range(1, NZ):
        pl.semaphore_signal(barrier, inc=1, device_id=zpeer(r), device_id_type=MESH)

    load_lat = pltpu.make_async_copy(starts_hbm, lat, local_sem.at[0])
    load_lat.start()
    own = pl.ds(pl.multiple_of(x * cols, cols), cols)
    load_mod = pltpu.make_async_copy(mod_hbm.at[:, :, own], mod, local_sem.at[1])
    load_mod.start()
    load_wq, load_wo = [], []
    for d in range(NX):
        block = pl.ds(pl.multiple_of(lax.rem(x + d, NX) * cols, cols), cols)
        load_wq.append(
            pltpu.make_async_copy(wq_hbm.at[:, block, :], wq.at[d], local_sem.at[2 + d])
        )
    for d in range(NX):
        block = pl.ds(pl.multiple_of(lax.rem(x + d, NX) * cols, cols), cols)
        load_wo.append(
            pltpu.make_async_copy(wo_hbm.at[:, block], wo.at[d], local_sem.at[6 + d])
        )
    for load in load_wq + load_wo:
        load.start()

    load_lat.wait()
    latent = lat[...]
    mean_here = jnp.mean(latent, axis=1, keepdims=True)
    away = latent - mean_here
    square_here = jnp.sum(away * away, axis=1, keepdims=True)
    lane = lax.broadcasted_iota(jnp.int32, (tokens, 128), 1)
    packed = jnp.where(lane == 0, mean_here, jnp.where(lane == 1, square_here, 0.0))
    st[0] = jnp.transpose(packed)[0:8, :]

    pl.semaphore_wait(barrier, (NX - 1) + (NQ - 1) + (NZ - 1))

    stat_copies = [cp.remote(st.at[0], st.at[NX - d], xpeer(d)) for d in range(1, NX)]
    for c in stat_copies:
        c.start()

    s0_a = [
        cp.remote(
            lat.at[pl.ds(pl.multiple_of(lax.rem(q + r, NQ) * rows, rows), rows), :], s0p, qpeer(r)
        )
        for r in range(1, NQ)
    ]

    @pl.when(tm == 0)
    def _():
        for c in s0_a:
            c.start()
        s0p[...] = lat[0:rows, :]

    for c in stat_copies:
        c.wait_recv()
    stats = [st[d] for d in range(NX)]
    mean_row = (stats[0][0:1] + stats[1][0:1] + stats[2][0:1] + stats[3][0:1]) / NX
    square_row = jnp.zeros_like(mean_row)
    for d in range(NX):
        shift = stats[d][0:1] - mean_row
        square_row += stats[d][1:2] + cols * (shift * shift)
    scale_row = lax.rsqrt(square_row / (cols * NX) + EPSILON)
    sub = lax.broadcasted_iota(jnp.int32, (128, tokens), 0)
    columns = jnp.transpose(jnp.where(sub == 0, mean_row, jnp.where(sub == 1, scale_row, 0.0)))
    mean_col, scale_col = columns[:, 0:1], columns[:, 1:2]
    load_mod.wait()
    normed = (lat[...] - mean_col) * scale_col
    xin[0] = (normed * (1.0 + mod[1]) + mod[0]).astype(jnp.bfloat16)

    in_copies = {d: cp.remote(xin.at[0], xin.at[NX - d], xpeer(d)) for d in (2, 1, 3)}
    for d in (2, 1, 3):
        in_copies[d].start()

    s0_b = [cp.remote(s0p, s0p, zpeer(r)) for r in range(1, NZ)]

    @pl.when(z == 0)
    def _():
        for i, c in enumerate(s0_a):

            @pl.when(q == i + 1)
            def _():
                c.wait_recv()

        for c in s0_b:
            c.start()

    def project(d, first):
        for j in range(3):
            part = jnp.dot(xin[d], wq[d, j], preferred_element_type=jnp.float32)
            acc[j] = part if first else acc[j] + part

    load_wq[0].wait()
    project(0, True)
    for d in (1, 3, 2):
        load_wq[d].wait()
        in_copies[NX - d].wait_recv()
        project(d, False)

    for h in range(acc.shape[2] // HEAD):
        here = slice(h * HEAD, (h + 1) * HEAD)

        def normal(j):
            t = acc[j, :, here]
            scale = lax.rsqrt(jnp.mean(t * t, axis=-1, keepdims=True) + EPSILON)
            return t * scale * gain_ref[j : j + 1, :]

        scores = lax.dot_general(
            normal(0), normal(1), (((1,), (1,)), ((), ())),
            precision=lax.Precision.HIGHEST, preferred_element_type=jnp.float32,
        ) * (HEAD ** -0.5)
        top = jnp.max(scores, axis=-1, keepdims=True)
        weight = jnp.exp(scores - top)
        probs = (weight / jnp.sum(weight, axis=-1, keepdims=True)).astype(jnp.bfloat16)
        values = acc[2, :, here].astype(jnp.bfloat16)
        heads[:, here] = jnp.dot(probs, values, preferred_element_type=jnp.float32).astype(
            jnp.bfloat16
        )

    for load in load_wo:
        load.wait()
    part_copies = []
    for p in range(PARTS):
        at = slice(p * half, (p + 1) * half)
        copies = {}
        for d in (2, 1, 3):
            psend[p, d] = jnp.dot(
                heads[...], wo[d, :, at], preferred_element_type=jnp.float32
            ).astype(jnp.bfloat16)
            copies[d] = cp.remote(psend.at[p, d], precv.at[p, NX - d], xpeer(d))
            copies[d].start()
        part_copies.append(copies)

    @pl.when(z != 0)
    def _():
        for i, c in enumerate(s0_b):

            @pl.when(z == i + 1)
            def _():
                c.wait_recv()

    mine = pl.ds(pl.multiple_of(q * rows, rows), rows)
    s0_c = [cp.remote(s0p, s0.at[mine, :], qpeer(r)) for r in range(1, NQ)]
    for c in s0_c:
        c.start()
    s0[mine, :] = s0p[...]

    position = (off_ref[0] + tm).astype(jnp.float32)

    def noise_level(at):
        fraction = 1.0 - jnp.full((8, 128), at, jnp.float32) / (3.0 * NQ * NZ)
        return 3.0 * fraction / (1.0 + 2.0 * fraction)

    step_size = (noise_level(position + 1.0) - noise_level(position))[0:1, 0:1]

    a_copies, out_copies = [], []
    for p in range(PARTS):
        at = slice(p * half, (p + 1) * half)
        attended = jnp.dot(heads[...], wo[0, :, at], preferred_element_type=jnp.float32)
        for d in (1, 3, 2):
            part_copies[p][NX - d].wait_recv()
            attended += precv[p, d].astype(jnp.float32)
        drift_here = lat[:, at] + mod[2][:, at] * attended
        drift[p] = drift_here
        c_here = step_size * drift_here
        cown[p] = c_here
        csend[p] = c_here.astype(jnp.bfloat16)
        copies = []
        for r in range(1, NQ):
            there = pl.ds(pl.multiple_of(lax.rem(q + r, NQ) * rows, rows), rows)
            copies.append(cp.remote(csend.at[p, there, :], arecv.at[p, q], qpeer(r)))
            copies[-1].start()
        arecv[p, q] = csend[p, mine, :]
        a_copies.append(copies)
        out_copies.append(
            pltpu.make_async_copy(drift.at[p], drift_hbm.at[:, at], local_sem.at[10 + p])
        )
        out_copies[-1].start()

    b_copies = []
    for p in range(PARTS):
        for c in a_copies[p]:
            c.wait_recv()
        total = jnp.zeros((rows, half), jnp.float32)
        for i in range(NQ):
            csum[p, i] = total
            total += arecv[p, i].astype(jnp.float32)
        bsend[p] = total.astype(jnp.bfloat16)
        copies = []
        for r in range(1, NZ):
            copies.append(cp.remote(bsend.at[p], brecv.at[p, r], zpeer(r)))

            @pl.when(z + r < NZ)
            def _():
                copies[-1].start()

        b_copies.append(copies)

    c_copies = []
    for p in range(PARTS):
        upd[p] = jnp.zeros((tokens, half), jnp.float32)
        for r in range(1, NZ):

            @pl.when(z >= r)
            def _():
                b_copies[p][r - 1].wait_recv()
                upd[p, 0:rows, :] += brecv[p, r].astype(jnp.float32)

        before = upd[p, 0:rows, :]
        for i in range(NQ):
            esend[p, i] = (before + csum[p, i]).astype(jnp.bfloat16)
        copies = []
        for r in range(1, NQ):
            copies.append(
                cp.remote(esend.at[p, lax.rem(q + r, NQ)], erecv.at[p, mine, :], qpeer(r))
            )
            copies[-1].start()
        erecv[p, mine, :] = esend[p, q]
        c_copies.append(copies)

    for c in s0_c:
        c.wait_recv()
    squared = jnp.zeros((1, 1), jnp.float32)
    for p in range(PARTS):
        at = slice(p * half, (p + 1) * half)
        for c in c_copies[p]:
            c.wait_recv()
        fresh = s0[:, at] + erecv[p].astype(jnp.float32)
        upd[p] = fresh + cown[p]
        out_copies.append(
            pltpu.make_async_copy(upd.at[p], upd_hbm.at[:, at], local_sem.at[12 + p])
        )
        out_copies[-1].start()
        change = fresh - lat[:, at]
        squared += jnp.sum(jnp.sum(change * change, axis=1, keepdims=True), axis=0, keepdims=True)
    rs[0] = jnp.broadcast_to(squared, (8, 128))
    r_copies = [cp.remote(rs.at[0], rs.at[NX - d], xpeer(d)) for d in range(1, NX)]
    for c in r_copies:
        c.start()
    for c in r_copies:
        c.wait_recv()
    res_ref[...] = (rs[0] + rs[1] + rs[2] + rs[3]) / (tokens * cols * NX)

    for c in out_copies:
        c.wait()
    sent = stat_copies + list(in_copies.values()) + s0_c + r_copies
    for copies in part_copies:
        sent += list(copies.values())
    for copies in a_copies + c_copies:
        sent += copies
    for c in sent:
        c.wait_send()

    @pl.when(tm == 0)
    def _():
        for c in s0_a:
            c.wait_send()

    @pl.when(z == 0)
    def _():
        for c in s0_b:
            c.wait_send()

    for r in range(1, NZ):

        @pl.when(z + r < NZ)
        def _():
            for p in range(PARTS):
                b_copies[p][r - 1].wait_send()


def body(starts, modulation, w_qkv, norm_gain, w_out, offset):
    tokens, cols = starts.shape[1:]
    inner = w_out.shape[0]
    half = cols // PARTS
    rows = tokens // NQ
    f32, bf16 = jnp.float32, jnp.bfloat16
    hbm = pl.BlockSpec(memory_space=pl.ANY)
    vmem = pl.BlockSpec(memory_space=pltpu.VMEM)
    updated, drift, residual = pl.pallas_call(
        kernel,
        out_shape=(
            jax.ShapeDtypeStruct((tokens, cols), f32),
            jax.ShapeDtypeStruct((tokens, cols), f32),
            jax.ShapeDtypeStruct((8, 128), f32),
        ),
        in_specs=[hbm, hbm, hbm, vmem, hbm, pl.BlockSpec(memory_space=pltpu.SMEM)],
        out_specs=(hbm, hbm, vmem),
        scratch_shapes=[
            pltpu.VMEM((tokens, cols), f32),
            pltpu.VMEM((3, 1, cols), f32),
            pltpu.VMEM((NX, 3, cols, inner), bf16),
            pltpu.VMEM((NX, inner, cols), bf16),
            pltpu.VMEM((NX, 8, 128), f32),
            pltpu.VMEM((NX, tokens, cols), bf16),
            pltpu.VMEM((3, tokens, inner), f32),
            pltpu.VMEM((tokens, inner), bf16),
            pltpu.VMEM((PARTS, NX, tokens, half), bf16),
            pltpu.VMEM((PARTS, NX, tokens, half), bf16),
            pltpu.VMEM((rows, cols), f32),
            pltpu.VMEM((tokens, cols), f32),
            pltpu.VMEM((PARTS, tokens, half), bf16),
            pltpu.VMEM((PARTS, NQ, rows, half), bf16),
            pltpu.VMEM((PARTS, rows, half), bf16),
            pltpu.VMEM((PARTS, NZ, rows, half), bf16),
            pltpu.VMEM((PARTS, NQ, rows, half), f32),
            pltpu.VMEM((PARTS, NQ, rows, half), bf16),
            pltpu.VMEM((PARTS, tokens, half), bf16),
            pltpu.VMEM((PARTS, tokens, half), f32),
            pltpu.VMEM((PARTS, tokens, half), f32),
            pltpu.VMEM((PARTS, tokens, half), f32),
            pltpu.VMEM((NX, 8, 128), f32),
            pltpu.SemaphoreType.DMA((14,)),
            pltpu.SemaphoreType.DMA((REMOTE,)),
            pltpu.SemaphoreType.DMA((REMOTE,)),
        ],
        compiler_params=pltpu.CompilerParams(
            collective_id=0, has_side_effects=True, vmem_limit_bytes=40 * 1024 * 1024
        ),
        name="sweep",
    )(
        starts.reshape(tokens, cols),
        modulation.transpose(1, 0, 2),
        w_qkv.transpose(1, 0, 2),
        norm_gain,
        w_out,
        offset,
    )
    return (updated[None], drift[None], residual[0, 0:1])


def solution(mesh):
    in_specs = (
        P("tm", None, "tp"),
        P("tm", None, None),
        P(None, None, "tp"),
        P(),
        P("tp", None),
        P(),
    )
    out_specs = (P("tm", None, "tp"), P("tm", None, "tp"), P("tm"))
    return jax.shard_map(body, mesh=mesh, in_specs=in_specs, out_specs=out_specs, check_vma=False)
```

time: 319 us -> 62.1 us (0.19)
  the two profiles are of different devices: /device:TPU:248 before, /device:TPU:32 now
where the time goes in v1:
time: 62.1 us; the launch traced here: 61.6 us
  Pallas kernels  51.2 us (82%)
  local copies, waits for them, and re-layouts  9.14 us (15%)
  between operations  1.3 us (2%)
    pallas_call x1, Pallas kernels, body(): pl.pallas_call(kernel, out_shape=(jax.ShapeDtypeStruct((tokens, cols), f3...  51.2 us
    unnamed x12, local copies, waits for them, and re-layouts  8.62 us

profile of v1, /device:TPU:32, one launch (start us, length us, event | category | flops | bytes accessed | tf_op | source)
XLA Modules:
  0.0 61.6 jit_solution(17197121607446038647)
XLA Ops:
  1.3 0.0 copy-start
  1.3 3.0 %copy-done = bf16[3072,3,384]{2,0,1:T(8,128)(2,1)S(1)} copy-done((bf16[3072,3,384]{2,0,1:T(8,128)(2,1)S(1)}, bf16[3072,3,384]{2,0,1:T(8,128)(2,1)}, u32[]{:S(2)}) %copy-start) | copy-done | bytes 7077912
  4.3 0.0 copy-start.1
  4.3 1.7 %copy-done.1 = bf16[384,3072]{1,0:T(8,128)(2,1)S(1)} copy-done((bf16[384,3072]{1,0:T(8,128)(2,1)S(1)}, bf16[384,3072]{1,0:T(8,128)(2,1)}, u32[]{:S(2)}) %copy-start.1) | copy-done | bytes 2359320
  6.0 0.0 copy-start.2
  6.0 1.0 %copy-done.2 = f32[1,128,768]{2,1,0:T(8,128)S(1)} copy-done((f32[1,128,768]{2,1,0:T(8,128)S(1)}, f32[1,128,768]{2,1,0:T(8,128)}, u32[]{:S(2)}) %copy-start.2) | copy-done | bytes 393240
  7.0 0.0 copy-start.3
  7.0 0.8 %copy-done.3 = f32[1,3,3072]{2,0,1:T(1,128)S(1)} copy-done((f32[1,3,3072]{2,0,1:T(1,128)S(1)}, f32[1,3,3072]{2,0,1:T(1,128)}, u32[]{:S(2)}) %copy-start.3) | copy-done | bytes 36888
  7.7 0.0 copy-start.4
  7.7 0.7 %copy-done.4 = f32[2,128]{1,0:T(2,128)S(1)} copy-done((f32[2,128]{1,0:T(2,128)S(1)}, f32[2,128]{1,0:T(2,128)}, u32[]{:S(2)}) %copy-start.4) | copy-done | bytes 1048
  8.4 51.2 %sweep.1 = (f32[128,768]{1,0:T(8,128)S(1)}, f32[128,768]{1,0:T(8,128)S(1)}, f32[8,128]{1,0:T(8,128)S(1)}) custom-call(f32[128,768]{1,0:T(8,128)S(1)} %bitcast.7, f32[3,1,3072]{2,1,0:T(1,128)S(1)} %bitcast.10, bf16[3,3072,384]{2,1,0:T(8,128)(2,1)S(1)} %bitcast.6, f32[2,128]{1,0:T(2,128)S(1)} %copy-done.4, bf16[384,3072]{1,0:T(8,128)(2,1)S(1)} %copy-done.1, ...), custom_call_target="tpu_custom_call" | custom-call | tf_op jit(solution)/shard_map/sweep/pallas_call | solution.py:345
  59.6 0.5 slice.3
  60.2 0.7 %copy.12 = f32[1,128,768]{2,1,0:T(8,128)} copy(f32[1,128,768]{2,1,0:T(8,128)S(1)} %bitcast.9) | data formatting | bytes 786432
  60.9 0.7 %copy.13 = f32[1,128,768]{2,1,0:T(8,128)} copy(f32[1,128,768]{2,1,0:T(8,128)S(1)} %bitcast.8) | data formatting | bytes 786432
Async XLA Ops:
  1.3 3.0 %copy-start = (bf16[3072,3,384]{2,0,1:T(8,128)(2,1)S(1)}, bf16[3072,3,384]{2,0,1:T(8,128)(2,1)}, u32[]{:S(2)}) copy-start(bf16[3072,3,384]{2,0,1:T(8,128)(2,1)} %param.8) | copy-start | bytes 21233668
  4.3 1.7 %copy-start.1 = (bf16[384,3072]{1,0:T(8,128)(2,1)S(1)}, bf16[384,3072]{1,0:T(8,128)(2,1)}, u32[]{:S(2)}) copy-start(bf16[384,3072]{1,0:T(8,128)(2,1)} %wo_hbm.1) | copy-start | bytes 7077892
  6.0 1.0 %copy-start.2 = (f32[1,128,768]{2,1,0:T(8,128)S(1)}, f32[1,128,768]{2,1,0:T(8,128)}, u32[]{:S(2)}) copy-start(f32[1,128,768]{2,1,0:T(8,128)} %param.6) | copy-start | bytes 1179652
  7.0 0.8 %copy-start.3 = (f32[1,3,3072]{2,0,1:T(1,128)S(1)}, f32[1,3,3072]{2,0,1:T(1,128)}, u32[]{:S(2)}) copy-start(f32[1,3,3072]{2,0,1:T(1,128)} %param.7) | copy-start | bytes 110596
  7.7 0.7 %copy-start.4 = (f32[2,128]{1,0:T(2,128)S(1)}, f32[2,128]{1,0:T(2,128)}, u32[]{:S(2)}) copy-start(f32[2,128]{1,0:T(2,128)} %gain_ref.1) | copy-start | bytes 3076

commit v2 on v1

--- a/solution.py
+++ b/solution.py
@@ -340,7 +340,7 @@
     half = cols // PARTS
     rows = tokens // NQ
     f32, bf16 = jnp.float32, jnp.bfloat16
-    hbm = pl.BlockSpec(memory_space=pl.ANY)
+    hbm = pl.BlockSpec(memory_space=pltpu.HBM)
     vmem = pl.BlockSpec(memory_space=pltpu.VMEM)
     updated, drift, residual = pl.pallas_call(
         kernel,
@@ -380,7 +380,7 @@
             pltpu.SemaphoreType.DMA((REMOTE,)),
         ],
         compiler_params=pltpu.CompilerParams(
-            collective_id=0, has_side_effects=True, vmem_limit_bytes=40 * 1024 * 1024
+            collective_id=0, has_side_effects=True, vmem_limit_bytes=60 * 1024 * 1024
         ),
         name="sweep",
     )(

time: 62.1 us -> 58.8 us (0.947)
  local copies, waits for them, and re-layouts: 9.14 us -> 4.72 us
  Pallas kernels: 51.2 us -> 52.6 us
    unnamed x12 -> x2, local copies, waits for them, and re-layouts: 8.62 us -> 3.53 us
    pallas_call x1, Pallas kernels: 51.2 us -> 52.6 us  [body(): pl.pallas_call(kernel, out_shape=(jax.ShapeDtypeStruct((tokens, cols), f3...]
    slice x1, local copies, waits for them, and re-layouts: 0.51 us -> 1.19 us  [body(): return (updated[None], drift[None], residual[0, 0:1])]
where the time goes in v2:
time: 58.8 us; the launch traced here: 58.6 us
  Pallas kernels  52.6 us (89%)
  local copies, waits for them, and re-layouts  4.72 us (8%)
  between operations  1.29 us (2%)
    pallas_call x1, Pallas kernels, body(): pl.pallas_call(kernel, out_shape=(jax.ShapeDtypeStruct((tokens, cols), f3...  52.6 us
    unnamed x2, local copies, waits for them, and re-layouts  3.53 us
    slice x1, local copies, waits for them, and re-layouts, body(): return (updated[None], drift[None], residual[0, 0:1])  1.19 us

profile of v2, /device:TPU:32, one launch (start us, length us, event | category | flops | bytes accessed | tf_op | source)
XLA Modules:
  0.0 58.6 jit_solution(1607806507677807711)
XLA Ops:
  1.3 52.6 %sweep.1 = (f32[128,768]{1,0:T(8,128)}, f32[128,768]{1,0:T(8,128)}, f32[8,128]{1,0:T(8,128)}) custom-call(f32[128,768]{1,0:T(8,128)} %bitcast.7, f32[3,1,3072]{2,1,0:T(1,128)} %bitcast.10, bf16[3,3072,384]{2,1,0:T(8,128)(2,1)} %bitcast.6, f32[2,128]{1,0:T(2,128)} %gain_ref.1, bf16[384,3072]{1,0:T(8,128)(2,1)} %wo_hbm.1, s32[1]{0:T(128)S(6)} %copy.11.off_ref), custom_call_target="tpu_custom_call" | custom-call | tf_op jit(solution)/shard_map/sweep/pallas_call | solution.py:345
  53.9 1.2 %slice.3 = f32[1,1]{1,0:T(1,128)} slice(f32[8,128]{1,0:T(8,128)} %get-tuple-element.8), slice={[0:1], [0:1]} | slice | bytes 8 | tf_op jit(solution)/shard_map/slice | solution.py:394
  55.1 1.8 %copy.12 = f32[1,128,768]{2,1,0:T(8,128)} copy(f32[1,128,768]{2,1,0:T(8,128)} %bitcast.9) | data formatting | bytes 786432
  56.8 1.8 %copy.13 = f32[1,128,768]{2,1,0:T(8,128)} copy(f32[1,128,768]{2,1,0:T(8,128)} %bitcast.8) | data formatting | bytes 786432

commit v3 on v2

--- a/solution.py
+++ b/solution.py
@@ -34,14 +34,14 @@
         )
 
 
-REMOTE = 3 + 3 + 7 + 7 + 7 + PARTS * (3 + 7 + 7 + 7) + 3
+REMOTE = 3 + 6 + 7 + 7 + 7 + 7 + PARTS * (3 + 7 + 7 + 7) + 31
 
 
 def kernel(
     starts_hbm, mod_hbm, wq_hbm, gain_ref, wo_hbm, off_ref,
-    upd_hbm, drift_hbm, res_ref,
+    upd_ref, drift_ref, res_ref,
     lat, mod, wq, wo, st, xin, acc, heads, psend, precv, s0p, s0,
-    csend, arecv, bsend, brecv, csum, esend, erecv, cown, drift, upd, rs,
+    csend, arecv, bsend, brecv, csum, esend, erecv, cown, zsum, latp, rsend, rrecv,
     local_sem, send_sem, recv_sem,
 ):
     tokens, cols = lat.shape
@@ -59,14 +59,16 @@
     def qpeer(r):
         return (z * NQ + lax.rem(q + r, NQ), x)
 
+    def xqpeer(d, r):
+        return (z * NQ + lax.rem(q + r, NQ), lax.rem(x + d, NX))
+
     def zpeer(r):
         return (lax.rem(z + r, NZ) * NQ + q, x)
 
+    near = [(d, r) for d in range(NX) for r in range(NQ) if d or r]
     barrier = pltpu.get_barrier_semaphore()
-    for d in range(1, NX):
-        pl.semaphore_signal(barrier, inc=1, device_id=xpeer(d), device_id_type=MESH)
-    for r in range(1, NQ):
-        pl.semaphore_signal(barrier, inc=1, device_id=qpeer(r), device_id_type=MESH)
+    for d, r in near:
+        pl.semaphore_signal(barrier, inc=1, device_id=xqpeer(d, r), device_id_type=MESH)
     for r in range(1, NZ):
         pl.semaphore_signal(barrier, inc=1, device_id=zpeer(r), device_id_type=MESH)
 
@@ -98,7 +100,7 @@
     packed = jnp.where(lane == 0, mean_here, jnp.where(lane == 1, square_here, 0.0))
     st[0] = jnp.transpose(packed)[0:8, :]
 
-    pl.semaphore_wait(barrier, (NX - 1) + (NQ - 1) + (NZ - 1))
+    pl.semaphore_wait(barrier, len(near) + (NZ - 1))
 
     stat_copies = [cp.remote(st.at[0], st.at[NX - d], xpeer(d)) for d in range(1, NX)]
     for c in stat_copies:
@@ -131,11 +133,24 @@
     mean_col, scale_col = columns[:, 0:1], columns[:, 1:2]
     load_mod.wait()
     normed = (lat[...] - mean_col) * scale_col
-    xin[0] = (normed * (1.0 + mod[1]) + mod[0]).astype(jnp.bfloat16)
-
-    in_copies = {d: cp.remote(xin.at[0], xin.at[NX - d], xpeer(d)) for d in (2, 1, 3)}
-    for d in (2, 1, 3):
-        in_copies[d].start()
+    modin = (normed * (1.0 + mod[1]) + mod[0]).astype(jnp.bfloat16)
+    deep = cols // 2
+    for k in range(2):
+        xin[0, k] = modin[:, k * deep : (k + 1) * deep]
+
+    to_right = [cp.remote(xin.at[0, k], xin.at[3, k], xpeer(1)) for k in range(2)]
+    to_left = [cp.remote(xin.at[0, k], xin.at[1, k], xpeer(3)) for k in range(2)]
+    pass_right = cp.remote(xin.at[3, 0], xin.at[2, 0], xpeer(1))
+    pass_left = cp.remote(xin.at[1, 1], xin.at[2, 1], xpeer(3))
+    for c in (to_right[0], to_left[1], to_right[1], to_left[0]):
+        c.start()
+
+    lat_copies = []
+    for r in range(1, NQ):
+        there = pl.ds(pl.multiple_of(lax.rem(q + r, NQ) * rows, rows), rows)
+        lat_copies.append(cp.remote(lat.at[there, :], latp.at[q], qpeer(r)))
+        lat_copies[-1].start()
+    latp[q] = lat[pl.ds(pl.multiple_of(q * rows, rows), rows), :]
 
     s0_b = [cp.remote(s0p, s0p, zpeer(r)) for r in range(1, NZ)]
 
@@ -150,17 +165,34 @@
         for c in s0_b:
             c.start()
 
-    def project(d, first):
+    def project(d, k, first=False):
         for j in range(3):
-            part = jnp.dot(xin[d], wq[d, j], preferred_element_type=jnp.float32)
+            part = jnp.dot(
+                xin[d, k], wq[d, j, k * deep : (k + 1) * deep, :],
+                preferred_element_type=jnp.float32,
+            )
             acc[j] = part if first else acc[j] + part
 
     load_wq[0].wait()
-    project(0, True)
-    for d in (1, 3, 2):
-        load_wq[d].wait()
-        in_copies[NX - d].wait_recv()
-        project(d, False)
+    project(0, 0, True)
+    project(0, 1)
+    to_right[0].wait_recv()
+    pass_right.start()
+    to_left[1].wait_recv()
+    pass_left.start()
+    load_wq[3].wait()
+    project(3, 0)
+    load_wq[1].wait()
+    project(1, 1)
+    to_right[1].wait_recv()
+    project(3, 1)
+    to_left[0].wait_recv()
+    project(1, 0)
+    load_wq[2].wait()
+    pass_right.wait_recv()
+    project(2, 0)
+    pass_left.wait_recv()
+    project(2, 1)
 
     for h in range(acc.shape[2] // HEAD):
         here = slice(h * HEAD, (h + 1) * HEAD)
@@ -218,7 +250,7 @@
 
     step_size = (noise_level(position + 1.0) - noise_level(position))[0:1, 0:1]
 
-    a_copies, out_copies = [], []
+    a_copies = []
     for p in range(PARTS):
         at = slice(p * half, (p + 1) * half)
         attended = jnp.dot(heads[...], wo[0, :, at], preferred_element_type=jnp.float32)
@@ -226,7 +258,7 @@
             part_copies[p][NX - d].wait_recv()
             attended += precv[p, d].astype(jnp.float32)
         drift_here = lat[:, at] + mod[2][:, at] * attended
-        drift[p] = drift_here
+        drift_ref[:, at] = drift_here
         c_here = step_size * drift_here
         cown[p] = c_here
         csend[p] = c_here.astype(jnp.bfloat16)
@@ -237,10 +269,6 @@
             copies[-1].start()
         arecv[p, q] = csend[p, mine, :]
         a_copies.append(copies)
-        out_copies.append(
-            pltpu.make_async_copy(drift.at[p], drift_hbm.at[:, at], local_sem.at[10 + p])
-        )
-        out_copies[-1].start()
 
     b_copies = []
     for p in range(PARTS):
@@ -261,19 +289,26 @@
 
         b_copies.append(copies)
 
+    for c in lat_copies:
+        c.wait_recv()
     c_copies = []
+    squares = [jnp.zeros((rows, half), jnp.float32) for _ in range(NQ)]
     for p in range(PARTS):
-        upd[p] = jnp.zeros((tokens, half), jnp.float32)
+        at = slice(p * half, (p + 1) * half)
+        zsum[p] = jnp.zeros((rows, half), jnp.float32)
         for r in range(1, NZ):
 
             @pl.when(z >= r)
             def _():
                 b_copies[p][r - 1].wait_recv()
-                upd[p, 0:rows, :] += brecv[p, r].astype(jnp.float32)
-
-        before = upd[p, 0:rows, :]
+                zsum[p] += brecv[p, r].astype(jnp.float32)
+
+        before = zsum[p]
         for i in range(NQ):
-            esend[p, i] = (before + csum[p, i]).astype(jnp.bfloat16)
+            entry = before + csum[p, i]
+            esend[p, i] = entry.astype(jnp.bfloat16)
+            change = s0p[:, at] + entry - latp[i, :, at]
+            squares[i] += change * change
         copies = []
         for r in range(1, NQ):
             copies.append(
@@ -283,32 +318,29 @@
         erecv[p, mine, :] = esend[p, q]
         c_copies.append(copies)
 
+    for i in range(NQ):
+        share = jnp.sum(jnp.sum(squares[i], axis=1, keepdims=True), axis=0, keepdims=True)
+        rsend[i] = jnp.broadcast_to(share, (8, 128))
+    r_copies = []
+    for d, r in near:
+        r_copies.append(
+            cp.remote(rsend.at[lax.rem(q + r, NQ)], rrecv.at[(NX - d) % NX, q], xqpeer(d, r))
+        )
+        r_copies[-1].start()
+    rrecv[0, q] = rsend[q]
+
     for c in s0_c:
         c.wait_recv()
-    squared = jnp.zeros((1, 1), jnp.float32)
     for p in range(PARTS):
         at = slice(p * half, (p + 1) * half)
         for c in c_copies[p]:
             c.wait_recv()
-        fresh = s0[:, at] + erecv[p].astype(jnp.float32)
-        upd[p] = fresh + cown[p]
-        out_copies.append(
-            pltpu.make_async_copy(upd.at[p], upd_hbm.at[:, at], local_sem.at[12 + p])
-        )
-        out_copies[-1].start()
-        change = fresh - lat[:, at]
-        squared += jnp.sum(jnp.sum(change * change, axis=1, keepdims=True), axis=0, keepdims=True)
-    rs[0] = jnp.broadcast_to(squared, (8, 128))
-    r_copies = [cp.remote(rs.at[0], rs.at[NX - d], xpeer(d)) for d in range(1, NX)]
-    for c in r_copies:
-        c.start()
+        upd_ref[:, at] = s0[:, at] + erecv[p].astype(jnp.float32) + cown[p]
     for c in r_copies:
         c.wait_recv()
-    res_ref[...] = (rs[0] + rs[1] + rs[2] + rs[3]) / (tokens * cols * NX)
-
-    for c in out_copies:
-        c.wait()
-    sent = stat_copies + list(in_copies.values()) + s0_c + r_copies
+    res_ref[...] = jnp.sum(rrecv[...], axis=(0, 1)) / (tokens * cols * NX)
+
+    sent = stat_copies + to_right + to_left + [pass_right, pass_left] + lat_copies + s0_c + r_copies
     for copies in part_copies:
         sent += list(copies.values())
     for copies in a_copies + c_copies:
@@ -345,19 +377,19 @@
     updated, drift, residual = pl.pallas_call(
         kernel,
         out_shape=(
-            jax.ShapeDtypeStruct((tokens, cols), f32),
-            jax.ShapeDtypeStruct((tokens, cols), f32),
-            jax.ShapeDtypeStruct((8, 128), f32),
+            pltpu.VMEM((tokens, cols), f32),
+            pltpu.VMEM((tokens, cols), f32),
+            pltpu.VMEM((8, 128), f32),
         ),
         in_specs=[hbm, hbm, hbm, vmem, hbm, pl.BlockSpec(memory_space=pltpu.SMEM)],
-        out_specs=(hbm, hbm, vmem),
+        out_specs=(vmem, vmem, vmem),
         scratch_shapes=[
             pltpu.VMEM((tokens, cols), f32),
             pltpu.VMEM((3, 1, cols), f32),
             pltpu.VMEM((NX, 3, cols, inner), bf16),
             pltpu.VMEM((NX, inner, cols), bf16),
             pltpu.VMEM((NX, 8, 128), f32),
-            pltpu.VMEM((NX, tokens, cols), bf16),
+            pltpu.VMEM((NX, 2, tokens, cols // 2), bf16),
             pltpu.VMEM((3, tokens, inner), f32),
             pltpu.VMEM((tokens, inner), bf16),
             pltpu.VMEM((PARTS, NX, tokens, half), bf16),
@@ -372,10 +404,11 @@
             pltpu.VMEM((PARTS, NQ, rows, half), bf16),
             pltpu.VMEM((PARTS, tokens, half), bf16),
             pltpu.VMEM((PARTS, tokens, half), f32),
-            pltpu.VMEM((PARTS, tokens, half), f32),
-            pltpu.VMEM((PARTS, tokens, half), f32),
-            pltpu.VMEM((NX, 8, 128), f32),
-            pltpu.SemaphoreType.DMA((14,)),
+            pltpu.VMEM((PARTS, rows, half), f32),
+            pltpu.VMEM((NQ, rows, cols), f32),
+            pltpu.VMEM((NQ, 8, 128), f32),
+            pltpu.VMEM((NX, NQ, 8, 128), f32),
+            pltpu.SemaphoreType.DMA((10,)),
             pltpu.SemaphoreType.DMA((REMOTE,)),
             pltpu.SemaphoreType.DMA((REMOTE,)),
         ],

time: 58.8 us -> 50.4 us (0.86)
  Pallas kernels: 52.6 us -> 46.7 us
  local copies, waits for them, and re-layouts: 4.72 us -> 2 us
    pallas_call x1, Pallas kernels: 52.6 us -> 46.7 us  [body(): pl.pallas_call(kernel, out_shape=(pltpu.VMEM((tokens, cols), f32), pltpu....]
    unnamed x2, local copies, waits for them, and re-layouts: 3.53 us -> 1.49 us
    slice x1, local copies, waits for them, and re-layouts: 1.19 us -> 0.51 us  [body(): return (updated[None], drift[None], residual[0, 0:1])]
where the time goes in v3:
time: 50.4 us; the launch traced here: 50 us
  Pallas kernels  46.7 us (93%)
  local copies, waits for them, and re-layouts  2 us (4%)
  between operations  1.29 us (3%)
    pallas_call x1, Pallas kernels, body(): pl.pallas_call(kernel, out_shape=(pltpu.VMEM((tokens, cols), f32), pltpu....  46.7 us
    unnamed x2, local copies, waits for them, and re-layouts  1.49 us

profile of v3, /device:TPU:32, one launch (start us, length us, event | category | flops | bytes accessed | tf_op | source)
XLA Modules:
  0.0 50.0 jit_solution(7692016190716555111)
XLA Ops:
  1.3 46.7 %sweep.1 = (f32[128,768]{1,0:T(8,128)S(1)}, f32[128,768]{1,0:T(8,128)S(1)}, f32[8,128]{1,0:T(8,128)S(1)}) custom-call(f32[128,768]{1,0:T(8,128)} %bitcast.9, f32[3,1,3072]{2,1,0:T(1,128)} %bitcast.10, bf16[3,3072,384]{2,1,0:T(8,128)(2,1)} %bitcast.8, f32[2,128]{1,0:T(2,128)} %gain_ref.1, bf16[384,3072]{1,0:T(8,128)(2,1)} %wo_hbm.1, s32[1]{0:T(128)S(6)} %copy.13.off_ref), custom_call_target="tpu_custom_call" | custom-call | tf_op jit(solution)/shard_map/sweep/pallas_call | solution.py:377
  48.0 0.5 %slice.3 = f32[1,1]{1,0:T(1,128)} slice(f32[8,128]{1,0:T(8,128)S(1)} %get-tuple-element.8), slice={[0:1], [0:1]} | slice | bytes 8 | tf_op jit(solution)/shard_map/slice | solution.py:427
  48.5 0.7 %copy.11 = f32[1,128,768]{2,1,0:T(8,128)} copy(f32[1,128,768]{2,1,0:T(8,128)S(1)} %bitcast.7) | data formatting | bytes 786432
  49.3 0.7 %copy.12 = f32[1,128,768]{2,1,0:T(8,128)} copy(f32[1,128,768]{2,1,0:T(8,128)S(1)} %bitcast.6) | data formatting | bytes 786432

commit v4 on v3

--- a/solution.py
+++ b/solution.py
@@ -42,7 +42,7 @@
     upd_ref, drift_ref, res_ref,
     lat, mod, wq, wo, st, xin, acc, heads, psend, precv, s0p, s0,
     csend, arecv, bsend, brecv, csum, esend, erecv, cown, zsum, latp, rsend, rrecv,
-    local_sem, send_sem, recv_sem,
+    local_sem, send_sem, recv_sem, spread_sem,
 ):
     tokens, cols = lat.shape
     half = cols // PARTS
@@ -67,10 +67,18 @@
 
     near = [(d, r) for d in range(NX) for r in range(NQ) if d or r]
     barrier = pltpu.get_barrier_semaphore()
-    for d, r in near:
-        pl.semaphore_signal(barrier, inc=1, device_id=xqpeer(d, r), device_id_type=MESH)
-    for r in range(1, NZ):
-        pl.semaphore_signal(barrier, inc=1, device_id=zpeer(r), device_id_type=MESH)
+    greeted = [xqpeer(d, 0) for d in range(1, NX)] + [qpeer(r) for r in range(1, NQ)]
+    greeted += [zpeer(1), zpeer(NZ - 1)]
+    for device in greeted:
+        pl.semaphore_signal(barrier, inc=1, device_id=device, device_id_type=MESH)
+
+    def spread(n):
+        for device in (zpeer(1), zpeer(NZ - 1)):
+            pl.semaphore_signal(spread_sem.at[n], inc=1, device_id=device, device_id_type=MESH)
+
+    def heard(n):
+        pl.semaphore_wait(spread_sem.at[n], 2)
+
 
     load_lat = pltpu.make_async_copy(starts_hbm, lat, local_sem.at[0])
     load_lat.start()
@@ -100,8 +108,9 @@
     packed = jnp.where(lane == 0, mean_here, jnp.where(lane == 1, square_here, 0.0))
     st[0] = jnp.transpose(packed)[0:8, :]
 
-    pl.semaphore_wait(barrier, len(near) + (NZ - 1))
-
+    pl.semaphore_wait(barrier, len(greeted))
+
+    spread(0)
     stat_copies = [cp.remote(st.at[0], st.at[NX - d], xpeer(d)) for d in range(1, NX)]
     for c in stat_copies:
         c.start()
@@ -121,6 +130,8 @@
 
     for c in stat_copies:
         c.wait_recv()
+    heard(0)
+    spread(1)
     stats = [st[d] for d in range(NX)]
     mean_row = (stats[0][0:1] + stats[1][0:1] + stats[2][0:1] + stats[3][0:1]) / NX
     square_row = jnp.zeros_like(mean_row)
@@ -152,19 +163,6 @@
         lat_copies[-1].start()
     latp[q] = lat[pl.ds(pl.multiple_of(q * rows, rows), rows), :]
 
-    s0_b = [cp.remote(s0p, s0p, zpeer(r)) for r in range(1, NZ)]
-
-    @pl.when(z == 0)
-    def _():
-        for i, c in enumerate(s0_a):
-
-            @pl.when(q == i + 1)
-            def _():
-                c.wait_recv()
-
-        for c in s0_b:
-            c.start()
-
     def project(d, k, first=False):
         for j in range(3):
             part = jnp.dot(
@@ -176,10 +174,26 @@
     load_wq[0].wait()
     project(0, 0, True)
     project(0, 1)
+    heard(1)
+    spread(2)
     to_right[0].wait_recv()
     pass_right.start()
     to_left[1].wait_recv()
     pass_left.start()
+    heard(2)
+    s0_b = [cp.remote(s0p, s0p, zpeer(r)) for r in range(1, NZ)]
+
+    @pl.when(z == 0)
+    def _():
+        for i, c in enumerate(s0_a):
+
+            @pl.when(q == i + 1)
+            def _():
+                c.wait_recv()
+
+        for c in s0_b:
+            c.start()
+
     load_wq[3].wait()
     project(3, 0)
     load_wq[1].wait()
@@ -411,6 +425,7 @@
             pltpu.SemaphoreType.DMA((10,)),
             pltpu.SemaphoreType.DMA((REMOTE,)),
             pltpu.SemaphoreType.DMA((REMOTE,)),
+            pltpu.SemaphoreType.REGULAR((3,)),
         ],
         compiler_params=pltpu.CompilerParams(
             collective_id=0, has_side_effects=True, vmem_limit_bytes=60 * 1024 * 1024

time: 50.4 us -> 48.9 us (0.970)
  Pallas kernels: 46.7 us -> 45.2 us
    pallas_call x1, Pallas kernels: 46.7 us -> 45.2 us  [body(): pl.pallas_call(kernel, out_shape=(pltpu.VMEM((tokens, cols), f32), pltpu....]
where the time goes in v4:
time: 48.9 us; the launch traced here: 48.5 us
  Pallas kernels  45.2 us (92%)
  local copies, waits for them, and re-layouts  2 us (4%)
  between operations  1.29 us (3%)
    pallas_call x1, Pallas kernels, body(): pl.pallas_call(kernel, out_shape=(pltpu.VMEM((tokens, cols), f32), pltpu....  45.2 us
    unnamed x2, local copies, waits for them, and re-layouts  1.49 us

profile of v4, /device:TPU:32, one launch (start us, length us, event | category | flops | bytes accessed | tf_op | source)
XLA Modules:
  0.0 48.5 jit_solution(11054702118185966437)
XLA Ops:
  1.3 45.2 %sweep.1 = (f32[128,768]{1,0:T(8,128)S(1)}, f32[128,768]{1,0:T(8,128)S(1)}, f32[8,128]{1,0:T(8,128)S(1)}) custom-call(f32[128,768]{1,0:T(8,128)} %bitcast.9, f32[3,1,3072]{2,1,0:T(1,128)} %bitcast.10, bf16[3,3072,384]{2,1,0:T(8,128)(2,1)} %bitcast.8, f32[2,128]{1,0:T(2,128)} %gain_ref.1, bf16[384,3072]{1,0:T(8,128)(2,1)} %wo_hbm.1, s32[1]{0:T(128)S(6)} %copy.13.off_ref), custom_call_target="tpu_custom_call" | custom-call | tf_op jit(solution)/shard_map/sweep/pallas_call | solution.py:391
  46.5 0.5 %slice.3 = f32[1,1]{1,0:T(1,128)} slice(f32[8,128]{1,0:T(8,128)S(1)} %get-tuple-element.8), slice={[0:1], [0:1]} | slice | bytes 8 | tf_op jit(solution)/shard_map/slice | solution.py:442
  47.0 0.7 %copy.11 = f32[1,128,768]{2,1,0:T(8,128)} copy(f32[1,128,768]{2,1,0:T(8,128)S(1)} %bitcast.7) | data formatting | bytes 786432
  47.8 0.7 %copy.12 = f32[1,128,768]{2,1,0:T(8,128)} copy(f32[1,128,768]{2,1,0:T(8,128)S(1)} %bitcast.6) | data formatting | bytes 786432

commit v5 on v4

--- a/solution.py
+++ b/solution.py
@@ -39,9 +39,9 @@
 
 def kernel(
     starts_hbm, mod_hbm, wq_hbm, gain_ref, wo_hbm, off_ref,
-    upd_ref, drift_ref, res_ref,
+    upd_ref, drift_ref, res_ref, step_ref,
     lat, mod, wq, wo, st, xin, acc, heads, psend, precv, s0p, s0,
-    csend, arecv, bsend, brecv, csum, esend, erecv, cown, zsum, latp, rsend, rrecv,
+    csend, arecv, bsend, brecv, csum, esend, erecv, zsum, latp, rsend, rrecv,
     local_sem, send_sem, recv_sem, spread_sem,
 ):
     tokens, cols = lat.shape
@@ -208,23 +208,26 @@
     pass_left.wait_recv()
     project(2, 1)
 
-    for h in range(acc.shape[2] // HEAD):
-        here = slice(h * HEAD, (h + 1) * HEAD)
-
-        def normal(j):
-            t = acc[j, :, here]
-            scale = lax.rsqrt(jnp.mean(t * t, axis=-1, keepdims=True) + EPSILON)
-            return t * scale * gain_ref[j : j + 1, :]
-
-        scores = lax.dot_general(
-            normal(0), normal(1), (((1,), (1,)), ((), ())),
+    places = [slice(h, h + HEAD) for h in range(0, heads.shape[1], HEAD)]
+
+    def normal(j, here):
+        t = acc[j, :, here]
+        scale = lax.rsqrt(jnp.mean(t * t, axis=-1, keepdims=True) + EPSILON)
+        return t * scale * gain_ref[j : j + 1, :]
+
+    pairs = [(normal(0, here), normal(1, here)) for here in places]
+    scores = [
+        lax.dot_general(
+            a, b, (((1,), (1,)), ((), ())),
             precision=lax.Precision.HIGHEST, preferred_element_type=jnp.float32,
         ) * (HEAD ** -0.5)
-        top = jnp.max(scores, axis=-1, keepdims=True)
-        weight = jnp.exp(scores - top)
-        probs = (weight / jnp.sum(weight, axis=-1, keepdims=True)).astype(jnp.bfloat16)
+        for a, b in pairs
+    ]
+    weights = [jnp.exp(t - jnp.max(t, axis=-1, keepdims=True)) for t in scores]
+    probs = [(t / jnp.sum(t, axis=-1, keepdims=True)).astype(jnp.bfloat16) for t in weights]
+    for here, t in zip(places, probs):
         values = acc[2, :, here].astype(jnp.bfloat16)
-        heads[:, here] = jnp.dot(probs, values, preferred_element_type=jnp.float32).astype(
+        heads[:, here] = jnp.dot(t, values, preferred_element_type=jnp.float32).astype(
             jnp.bfloat16
         )
 
@@ -264,6 +267,7 @@
 
     step_size = (noise_level(position + 1.0) - noise_level(position))[0:1, 0:1]
 
+    step_ref[...] = jnp.broadcast_to(step_size, step_ref.shape)
     a_copies = []
     for p in range(PARTS):
         at = slice(p * half, (p + 1) * half)
@@ -271,10 +275,10 @@
         for d in (1, 3, 2):
             part_copies[p][NX - d].wait_recv()
             attended += precv[p, d].astype(jnp.float32)
-        drift_here = lat[:, at] + mod[2][:, at] * attended
-        drift_ref[:, at] = drift_here
+        gated = mod[2][:, at] * attended
+        drift_ref[:, at] = gated
+        drift_here = lat[:, at] + gated
         c_here = step_size * drift_here
-        cown[p] = c_here
         csend[p] = c_here.astype(jnp.bfloat16)
         copies = []
         for r in range(1, NQ):
@@ -333,8 +337,8 @@
         c_copies.append(copies)
 
     for i in range(NQ):
-        share = jnp.sum(jnp.sum(squares[i], axis=1, keepdims=True), axis=0, keepdims=True)
-        rsend[i] = jnp.broadcast_to(share, (8, 128))
+        tiles = [squares[i][:, b : b + 128] for b in range(0, half, 128)]
+        rsend[i] = jnp.sum(sum(tiles[1:], tiles[0]), axis=0, keepdims=True)
     r_copies = []
     for d, r in near:
         r_copies.append(
@@ -349,10 +353,11 @@
         at = slice(p * half, (p + 1) * half)
         for c in c_copies[p]:
             c.wait_recv()
-        upd_ref[:, at] = s0[:, at] + erecv[p].astype(jnp.float32) + cown[p]
+        upd_ref[:, at] = s0[:, at] + erecv[p].astype(jnp.float32)
     for c in r_copies:
         c.wait_recv()
-    res_ref[...] = jnp.sum(rrecv[...], axis=(0, 1)) / (tokens * cols * NX)
+    squared = jnp.sum(jnp.sum(rrecv[...], axis=(0, 1)), axis=1, keepdims=True)
+    res_ref[...] = squared / (tokens * cols * NX)
 
     sent = stat_copies + to_right + to_left + [pass_right, pass_left] + lat_copies + s0_c + r_copies
     for copies in part_copies:
@@ -388,15 +393,16 @@
     f32, bf16 = jnp.float32, jnp.bfloat16
     hbm = pl.BlockSpec(memory_space=pltpu.HBM)
     vmem = pl.BlockSpec(memory_space=pltpu.VMEM)
-    updated, drift, residual = pl.pallas_call(
+    fresh, gated, residual, step = pl.pallas_call(
         kernel,
         out_shape=(
             pltpu.VMEM((tokens, cols), f32),
             pltpu.VMEM((tokens, cols), f32),
-            pltpu.VMEM((8, 128), f32),
+            pltpu.VMEM((1, 1), f32),
+            pltpu.VMEM((1, cols), f32),
         ),
         in_specs=[hbm, hbm, hbm, vmem, hbm, pl.BlockSpec(memory_space=pltpu.SMEM)],
-        out_specs=(vmem, vmem, vmem),
+        out_specs=(vmem, vmem, vmem, vmem),
         scratch_shapes=[
             pltpu.VMEM((tokens, cols), f32),
             pltpu.VMEM((3, 1, cols), f32),
@@ -417,11 +423,10 @@
             pltpu.VMEM((PARTS, NQ, rows, half), f32),
             pltpu.VMEM((PARTS, NQ, rows, half), bf16),
             pltpu.VMEM((PARTS, tokens, half), bf16),
-            pltpu.VMEM((PARTS, tokens, half), f32),
             pltpu.VMEM((PARTS, rows, half), f32),
             pltpu.VMEM((NQ, rows, cols), f32),
-            pltpu.VMEM((NQ, 8, 128), f32),
-            pltpu.VMEM((NX, NQ, 8, 128), f32),
+            pltpu.VMEM((NQ, 1, 128), f32),
+            pltpu.VMEM((NX, NQ, 1, 128), f32),
             pltpu.SemaphoreType.DMA((10,)),
             pltpu.SemaphoreType.DMA((REMOTE,)),
             pltpu.SemaphoreType.DMA((REMOTE,)),
@@ -439,7 +444,8 @@
         w_out,
         offset,
     )
-    return (updated[None], drift[None], residual[0, 0:1])
+    drift = starts + gated[None]
+    return (fresh[None] + step[None] * drift, drift, residual.reshape(1))
 
 
 def solution(mesh):

time: 48.9 us -> 47.6 us (0.973)
  local copies, waits for them, and re-layouts: 2 us -> 0.01 us
  between operations: 1.29 us -> 2.52 us
  Pallas kernels: 45.2 us -> 44 us
  other arithmetic: 0 us -> 0.96 us
    unnamed x2, local copies, waits for them, and re-layouts: 1.49 us -> 0.01 us
    pallas_call x1, Pallas kernels: 45.2 us -> 44 us  [body(): pl.pallas_call(kernel, out_shape=(pltpu.VMEM((tokens, cols), f32), pltpu....]
    add x0 -> x1, other arithmetic: none -> 0.95 us  [body(): return (fresh[None] + step[None] * drift, drift, residual.reshape(1))]
    slice x1 -> x0, local copies, waits for them, and re-layouts: 0.51 us -> none  [body(): return (updated[None], drift[None], residual[0, 0:1])]
where the time goes in v5:
time: 47.6 us; the launch traced here: 47.5 us
  Pallas kernels  44 us (92%)
  between operations  2.52 us (5%)
  other arithmetic  0.96 us (2%)
    pallas_call x1, Pallas kernels, body(): pl.pallas_call(kernel, out_shape=(pltpu.VMEM((tokens, cols), f32), pltpu....  44 us

profile of v5, /device:TPU:32, one launch (start us, length us, event | category | flops | bytes accessed | tf_op | source)
XLA Modules:
  0.0 47.5 jit_solution(13010062677227868086)
XLA Ops:
  0.6 0.0 copy-start
  1.3 44.0 %sweep.1 = (f32[128,768]{1,0:T(8,128)S(1)}, f32[128,768]{1,0:T(8,128)S(1)}, f32[1,1]{1,0:T(1,128)S(1)}, f32[1,768]{1,0:T(1,128)S(1)}) custom-call(f32[128,768]{1,0:T(8,128)} %bitcast.10, f32[3,1,3072]{2,1,0:T(1,128)} %bitcast.11, bf16[3,3072,384]{2,1,0:T(8,128)(2,1)} %bitcast.9, f32[2,128]{1,0:T(2,128)} %gain_ref.1, bf16[384,3072]{1,0:T(8,128)(2,1)} %wo_hbm.1, ...), custom_call_target="tpu_custom_call" | custom-call | tf_op jit(solution)/shard_map/sweep/pallas_call | solution.py:396
  45.4 0.0 copy-done
  45.4 0.9 %bitcast_add_fusion.1 = (f32[1,128,768]{2,1,0:T(8,128)}, f32[1,128,768]{2,1,0:T(8,128)}) fusion(f32[128,768]{1,0:T(8,128)S(1)} %get-tuple-element.7, f32[768]{0:T(1024)S(1)} %reduce, f32[1,128,768]{2,1,0:T(8,128)S(1)} %copy-done, f32[128,768]{1,0:T(8,128)S(1)} %get-tuple-element.9), kind=kLoop, calls=%fused_computation.1 | loop fusion | flops 294912 | bytes 1969152 | tf_op jit(solution)/shard_map/add | solution.py:448
  (1 shorter events, 0.0 us)
Async XLA Ops:
  0.6 44.7 %copy-start = (f32[1,128,768]{2,1,0:T(8,128)S(1)}, f32[1,128,768]{2,1,0:T(8,128)}, u32[]{:S(2)}) copy-start(f32[1,128,768]{2,1,0:T(8,128)} %param.6) | copy-start | bytes 1179652

commit v6 on v5

--- a/solution.py
+++ b/solution.py
@@ -33,14 +33,22 @@
             device_id_type=MESH,
         )
 
-
-REMOTE = 3 + 6 + 7 + 7 + 7 + 7 + PARTS * (3 + 7 + 7 + 7) + 31
+    def several(self, whole_src, whole_dst, copies):
+        at = self.used
+        for src, dst, device in copies:
+            self.used = at
+            self.remote(src, dst, device).start()
+        self.used = at
+        return self.remote(whole_src, whole_dst, device)
+
+
+REMOTE = 3 + 6 + 7 + 7 + 7 + 7 + PARTS * (3 + 1 + 7 + 1) + 1
 
 
 def kernel(
-    starts_hbm, mod_hbm, wq_hbm, gain_ref, wo_hbm, off_ref,
+    starts_hbm, mod_hbm, wq_hbm, gain_hbm, wo_hbm, off_hbm,
     upd_ref, drift_ref, res_ref, step_ref,
-    lat, mod, wq, wo, st, xin, acc, heads, psend, precv, s0p, s0,
+    lat, mod, off_ref, gain_ref, wq, wo, st, xin, acc, heads, psend, precv, s0p, s0,
     csend, arecv, bsend, brecv, csum, esend, erecv, zsum, latp, rsend, rrecv,
     local_sem, send_sem, recv_sem, spread_sem,
 ):
@@ -85,6 +93,10 @@
     own = pl.ds(pl.multiple_of(x * cols, cols), cols)
     load_mod = pltpu.make_async_copy(mod_hbm.at[:, :, own], mod, local_sem.at[1])
     load_mod.start()
+    load_gain = pltpu.make_async_copy(gain_hbm, gain_ref, local_sem.at[10])
+    load_gain.start()
+    load_off = pltpu.make_async_copy(off_hbm, off_ref, local_sem.at[11])
+    load_off.start()
     load_wq, load_wo = [], []
     for d in range(NX):
         block = pl.ds(pl.multiple_of(lax.rem(x + d, NX) * cols, cols), cols)
@@ -215,6 +227,8 @@
         scale = lax.rsqrt(jnp.mean(t * t, axis=-1, keepdims=True) + EPSILON)
         return t * scale * gain_ref[j : j + 1, :]
 
+    load_gain.wait()
+    load_off.wait()
     pairs = [(normal(0, here), normal(1, here)) for here in places]
     scores = [
         lax.dot_general(
@@ -283,15 +297,14 @@
         copies = []
         for r in range(1, NQ):
             there = pl.ds(pl.multiple_of(lax.rem(q + r, NQ) * rows, rows), rows)
-            copies.append(cp.remote(csend.at[p, there, :], arecv.at[p, q], qpeer(r)))
-            copies[-1].start()
+            copies.append((csend.at[p, there, :], arecv.at[p, q], qpeer(r)))
+        others = pl.ds(0, tokens - rows)
+        a_copies.append(cp.several(csend.at[p, others, :], arecv.at[p, 0 : NQ - 1], copies))
         arecv[p, q] = csend[p, mine, :]
-        a_copies.append(copies)
 
     b_copies = []
     for p in range(PARTS):
-        for c in a_copies[p]:
-            c.wait_recv()
+        a_copies[p].wait_recv()
         total = jnp.zeros((rows, half), jnp.float32)
         for i in range(NQ):
             csum[p, i] = total
@@ -307,6 +320,23 @@
 
         b_copies.append(copies)
 
+    sent = stat_copies + to_right + to_left + [pass_right, pass_left] + lat_copies + s0_c
+    for copies in part_copies:
+        sent += list(copies.values())
+    sent += a_copies
+    for c in sent:
+        c.wait_send()
+
+    @pl.when(tm == 0)
+    def _():
+        for c in s0_a:
+            c.wait_send()
+
+    @pl.when(z == 0)
+    def _():
+        for c in s0_b:
+            c.wait_send()
+
     for c in lat_copies:
         c.wait_recv()
     c_copies = []
@@ -327,55 +357,30 @@
             esend[p, i] = entry.astype(jnp.bfloat16)
             change = s0p[:, at] + entry - latp[i, :, at]
             squares[i] += change * change
-        copies = []
-        for r in range(1, NQ):
-            copies.append(
-                cp.remote(esend.at[p, lax.rem(q + r, NQ)], erecv.at[p, mine, :], qpeer(r))
-            )
-            copies[-1].start()
+        copies = [
+            (esend.at[p, lax.rem(q + r, NQ)], erecv.at[p, mine, :], qpeer(r))
+            for r in range(1, NQ)
+        ]
+        c_copies.append(cp.several(esend.at[p, 0 : NQ - 1], erecv.at[p, others, :], copies))
         erecv[p, mine, :] = esend[p, q]
-        c_copies.append(copies)
 
     for i in range(NQ):
         tiles = [squares[i][:, b : b + 128] for b in range(0, half, 128)]
         rsend[i] = jnp.sum(sum(tiles[1:], tiles[0]), axis=0, keepdims=True)
-    r_copies = []
-    for d, r in near:
-        r_copies.append(
-            cp.remote(rsend.at[lax.rem(q + r, NQ)], rrecv.at[(NX - d) % NX, q], xqpeer(d, r))
-        )
-        r_copies[-1].start()
-    rrecv[0, q] = rsend[q]
+    shares = rrecv.at[0 : len(near)]
+    r_all = cp.several(
+        shares, shares,
+        [
+            (rsend.at[lax.rem(q + r, NQ)], rrecv.at[n], xqpeer(d, r))
+            for n, (d, r) in enumerate(near)
+        ],
+    )
+    rrecv[len(near)] = rsend[q]
 
     for c in s0_c:
         c.wait_recv()
-    for p in range(PARTS):
-        at = slice(p * half, (p + 1) * half)
-        for c in c_copies[p]:
-            c.wait_recv()
-        upd_ref[:, at] = s0[:, at] + erecv[p].astype(jnp.float32)
-    for c in r_copies:
-        c.wait_recv()
-    squared = jnp.sum(jnp.sum(rrecv[...], axis=(0, 1)), axis=1, keepdims=True)
-    res_ref[...] = squared / (tokens * cols * NX)
-
-    sent = stat_copies + to_right + to_left + [pass_right, pass_left] + lat_copies + s0_c + r_copies
-    for copies in part_copies:
-        sent += list(copies.values())
-    for copies in a_copies + c_copies:
-        sent += copies
-    for c in sent:
+    for c in c_copies + [r_all]:
         c.wait_send()
-
-    @pl.when(tm == 0)
-    def _():
-        for c in s0_a:
-            c.wait_send()
-
-    @pl.when(z == 0)
-    def _():
-        for c in s0_b:
-            c.wait_send()
 
     for r in range(1, NZ):
 
@@ -383,6 +388,13 @@
         def _():
             for p in range(PARTS):
                 b_copies[p][r - 1].wait_send()
+    for p in range(PARTS):
+        at = slice(p * half, (p + 1) * half)
+        c_copies[p].wait_recv()
+        upd_ref[:, at] = s0[:, at] + erecv[p].astype(jnp.float32)
+    r_all.wait_recv()
+    squared = jnp.sum(jnp.sum(rrecv[...], axis=0), axis=1, keepdims=True)
+    res_ref[...] = squared / (tokens * cols * NX)
 
 
 def body(starts, modulation, w_qkv, norm_gain, w_out, offset):
@@ -401,11 +413,13 @@
             pltpu.VMEM((1, 1), f32),
             pltpu.VMEM((1, cols), f32),
         ),
-        in_specs=[hbm, hbm, hbm, vmem, hbm, pl.BlockSpec(memory_space=pltpu.SMEM)],
+        in_specs=[hbm, hbm, hbm, hbm, hbm, hbm],
         out_specs=(vmem, vmem, vmem, vmem),
         scratch_shapes=[
             pltpu.VMEM((tokens, cols), f32),
             pltpu.VMEM((3, 1, cols), f32),
+            pltpu.SMEM((1,), jnp.int32),
+            pltpu.VMEM((2, HEAD), f32),
             pltpu.VMEM((NX, 3, cols, inner), bf16),
             pltpu.VMEM((NX, inner, cols), bf16),
             pltpu.VMEM((NX, 8, 128), f32),
@@ -426,8 +440,8 @@
             pltpu.VMEM((PARTS, rows, half), f32),
             pltpu.VMEM((NQ, rows, cols), f32),
             pltpu.VMEM((NQ, 1, 128), f32),
-            pltpu.VMEM((NX, NQ, 1, 128), f32),
-            pltpu.SemaphoreType.DMA((10,)),
+            pltpu.VMEM((NX * NQ, 1, 128), f32),
+            pltpu.SemaphoreType.DMA((12,)),
             pltpu.SemaphoreType.DMA((REMOTE,)),
             pltpu.SemaphoreType.DMA((REMOTE,)),
             pltpu.SemaphoreType.REGULAR((3,)),

time: 47.6 us -> 46 us (0.966)
  Pallas kernels: 44 us -> 42.4 us
    pallas_call x1, Pallas kernels: 44 us -> 42.4 us  [body(): pl.pallas_call(kernel, out_shape=(pltpu.VMEM((tokens, cols), f32), pltpu....]
where the time goes in v6:
time: 46 us; the launch traced here: 45.9 us
  Pallas kernels  42.4 us (92%)
  between operations  2.52 us (5%)
  other arithmetic  0.96 us (2%)
    pallas_call x1, Pallas kernels, body(): pl.pallas_call(kernel, out_shape=(pltpu.VMEM((tokens, cols), f32), pltpu....  42.4 us
    add x1, other arithmetic, body(): return (fresh[None] + step[None] * drift, drift, residual.reshape(1))  0.95 us

profile of v6, /device:TPU:32, one launch (start us, length us, event | category | flops | bytes accessed | tf_op | source)
XLA Modules:
  0.0 45.9 jit_solution(18359679250159109343)
XLA Ops:
  0.6 0.0 copy-start
  1.3 42.4 %sweep.1 = (f32[128,768]{1,0:T(8,128)S(1)}, f32[128,768]{1,0:T(8,128)S(1)}, f32[1,1]{1,0:T(1,128)S(1)}, f32[1,768]{1,0:T(1,128)S(1)}) custom-call(f32[128,768]{1,0:T(8,128)} %bitcast.10, f32[3,1,3072]{2,1,0:T(1,128)} %bitcast.11, bf16[3,3072,384]{2,1,0:T(8,128)(2,1)} %bitcast.9, f32[2,128]{1,0:T(2,128)} %gain_hbm.1, bf16[384,3072]{1,0:T(8,128)(2,1)} %wo_hbm.1, ...), custom_call_target="tpu_custom_call" | custom-call | tf_op jit(solution)/shard_map/sweep/pallas_call | solution.py:408
  43.8 0.0 copy-done
  43.8 0.9 %bitcast_add_fusion.1 = (f32[1,128,768]{2,1,0:T(8,128)}, f32[1,128,768]{2,1,0:T(8,128)}) fusion(f32[128,768]{1,0:T(8,128)S(1)} %get-tuple-element.7, f32[768]{0:T(1024)S(1)} %reduce, f32[1,128,768]{2,1,0:T(8,128)S(1)} %copy-done, f32[128,768]{1,0:T(8,128)S(1)} %get-tuple-element.9), kind=kLoop, calls=%fused_computation.1 | loop fusion | flops 294912 | bytes 1969152 | tf_op jit(solution)/shard_map/add | solution.py:462
  (1 shorter events, 0.0 us)
Async XLA Ops:
  0.6 43.2 %copy-start = (f32[1,128,768]{2,1,0:T(8,128)S(1)}, f32[1,128,768]{2,1,0:T(8,128)}, u32[]{:S(2)}) copy-start(f32[1,128,768]{2,1,0:T(8,128)} %param.6) | copy-start | bytes 1179652

commit v7 on v6

--- a/solution.py
+++ b/solution.py
@@ -73,10 +73,10 @@
     def zpeer(r):
         return (lax.rem(z + r, NZ) * NQ + q, x)
 
-    near = [(d, r) for d in range(NX) for r in range(NQ) if d or r]
+    near = [(d, r) for d in (2, 1, 3, 0) for r in (4, 5, 3, 6, 2, 7, 1, 0) if d or r]
     barrier = pltpu.get_barrier_semaphore()
-    greeted = [xqpeer(d, 0) for d in range(1, NX)] + [qpeer(r) for r in range(1, NQ)]
-    greeted += [zpeer(1), zpeer(NZ - 1)]
+    greeted = [zpeer(1), zpeer(NZ - 1)] + [qpeer(r) for r in (4, 5, 3, 6, 2, 7, 1)]
+    greeted += [xpeer(d) for d in (2, 1, 3)]
     for device in greeted:
         pl.semaphore_signal(barrier, inc=1, device_id=device, device_id_type=MESH)
 
@@ -123,9 +123,10 @@
     pl.semaphore_wait(barrier, len(greeted))
 
     spread(0)
-    stat_copies = [cp.remote(st.at[0], st.at[NX - d], xpeer(d)) for d in range(1, NX)]
-    for c in stat_copies:
-        c.start()
+    tiles = st.at[1:NX]
+    stat_copies = [
+        cp.several(tiles, tiles, [(st.at[0], st.at[NX - d], xpeer(d)) for d in (2, 1, 3)])
+    ]
 
     s0_a = [
         cp.remote(
@@ -155,17 +156,22 @@
     columns = jnp.transpose(jnp.where(sub == 0, mean_row, jnp.where(sub == 1, scale_row, 0.0)))
     mean_col, scale_col = columns[:, 0:1], columns[:, 1:2]
     load_mod.wait()
-    normed = (lat[...] - mean_col) * scale_col
-    modin = (normed * (1.0 + mod[1]) + mod[0]).astype(jnp.bfloat16)
     deep = cols // 2
-    for k in range(2):
-        xin[0, k] = modin[:, k * deep : (k + 1) * deep]
+
+    def prepare(k):
+        part = slice(k * deep, (k + 1) * deep)
+        normed = (lat[:, part] - mean_col) * scale_col
+        modin = normed * (1.0 + mod[1][:, part]) + mod[0][:, part]
+        xin[0, k] = modin.astype(jnp.bfloat16)
 
     to_right = [cp.remote(xin.at[0, k], xin.at[3, k], xpeer(1)) for k in range(2)]
     to_left = [cp.remote(xin.at[0, k], xin.at[1, k], xpeer(3)) for k in range(2)]
     pass_right = cp.remote(xin.at[3, 0], xin.at[2, 0], xpeer(1))
     pass_left = cp.remote(xin.at[1, 1], xin.at[2, 1], xpeer(3))
-    for c in (to_right[0], to_left[1], to_right[1], to_left[0]):
+    prepare(0)
+    to_right[0].start()
+    prepare(1)
+    for c in (to_left[1], to_right[1], to_left[0]):
         c.start()
 
     lat_copies = []
@@ -186,39 +192,45 @@
     load_wq[0].wait()
     project(0, 0, True)
     project(0, 1)
-    heard(1)
-    spread(2)
     to_right[0].wait_recv()
     pass_right.start()
     to_left[1].wait_recv()
     pass_left.start()
-    heard(2)
-    s0_b = [cp.remote(s0p, s0p, zpeer(r)) for r in range(1, NZ)]
-
-    @pl.when(z == 0)
-    def _():
-        for i, c in enumerate(s0_a):
-
-            @pl.when(q == i + 1)
-            def _():
-                c.wait_recv()
-
-        for c in s0_b:
-            c.start()
-
+    heard(1)
+    spread(2)
     load_wq[3].wait()
     project(3, 0)
     load_wq[1].wait()
     project(1, 1)
+    heard(2)
+    s0_b = [cp.remote(s0p, s0p, zpeer(r)) for r in range(1, NZ)]
+
+    @pl.when(z == 0)
+    def _():
+        for i, c in enumerate(s0_a):
+
+            @pl.when(q == i + 1)
+            def _():
+                c.wait_recv()
+
+        for c in s0_b:
+            c.start()
+
     to_right[1].wait_recv()
     project(3, 1)
     to_left[0].wait_recv()
     project(1, 0)
     load_wq[2].wait()
     pass_right.wait_recv()
-    project(2, 0)
     pass_left.wait_recv()
-    project(2, 1)
+    for j in range(3):
+        acc[j] += sum(
+            jnp.dot(
+                xin[2, k], wq[2, j, k * deep : (k + 1) * deep, :],
+                preferred_element_type=jnp.float32,
+            )
+            for k in range(2)
+        )
 
     places = [slice(h, h + HEAD) for h in range(0, heads.shape[1], HEAD)]
 
@@ -339,6 +351,21 @@
 
     for c in lat_copies:
         c.wait_recv()
+    def send_squares():
+        for i in range(NQ):
+            tiles = [squares[i][:, b : b + 128] for b in range(0, half, 128)]
+            rsend[i] = jnp.sum(sum(tiles[1:], tiles[0]), axis=0, keepdims=True)
+        shares = rrecv.at[0 : len(near)]
+        r_all = cp.several(
+            shares, shares,
+            [
+                (rsend.at[lax.rem(q + r, NQ)], rrecv.at[n], xqpeer(d, r))
+                for n, (d, r) in enumerate(near)
+            ],
+        )
+        rrecv[len(near)] = rsend[q]
+        return r_all
+
     c_copies = []
     squares = [jnp.zeros((rows, half), jnp.float32) for _ in range(NQ)]
     for p in range(PARTS):
@@ -353,29 +380,18 @@
 
         before = zsum[p]
         for i in range(NQ):
-            entry = before + csum[p, i]
-            esend[p, i] = entry.astype(jnp.bfloat16)
-            change = s0p[:, at] + entry - latp[i, :, at]
+            change = s0p[:, at] + (before + csum[p, i]) - latp[i, :, at]
             squares[i] += change * change
+        if p == PARTS - 1:
+            r_all = send_squares()
+        for i in range(NQ):
+            esend[p, i] = (before + csum[p, i]).astype(jnp.bfloat16)
         copies = [
             (esend.at[p, lax.rem(q + r, NQ)], erecv.at[p, mine, :], qpeer(r))
             for r in range(1, NQ)
         ]
         c_copies.append(cp.several(esend.at[p, 0 : NQ - 1], erecv.at[p, others, :], copies))
         erecv[p, mine, :] = esend[p, q]
-
-    for i in range(NQ):
-        tiles = [squares[i][:, b : b + 128] for b in range(0, half, 128)]
-        rsend[i] = jnp.sum(sum(tiles[1:], tiles[0]), axis=0, keepdims=True)
-    shares = rrecv.at[0 : len(near)]
-    r_all = cp.several(
-        shares, shares,
-        [
-            (rsend.at[lax.rem(q + r, NQ)], rrecv.at[n], xqpeer(d, r))
-            for n, (d, r) in enumerate(near)
-        ],
-    )
-    rrecv[len(near)] = rsend[q]
 
     for c in s0_c:
         c.wait_recv()

time: 46 us -> 45.9 us (level)
  no operation moved by 1% of the time
where the time goes in v7:
time: 45.9 us; the launch traced here: 45.7 us
  Pallas kernels  42.2 us (92%)
  between operations  2.52 us (5%)
  other arithmetic  0.96 us (2%)
    pallas_call x1, Pallas kernels, body(): pl.pallas_call(kernel, out_shape=(pltpu.VMEM((tokens, cols), f32), pltpu....  42.2 us
    add x1, other arithmetic, body(): return (fresh[None] + step[None] * drift, drift, residual.reshape(1))  0.95 us

profile of v7, /device:TPU:32, one launch (start us, length us, event | category | flops | bytes accessed | tf_op | source)
XLA Modules:
  0.0 45.7 jit_solution(6283255463539375101)
XLA Ops:
  0.6 0.0 copy-start
  1.3 42.2 %sweep.1 = (f32[128,768]{1,0:T(8,128)S(1)}, f32[128,768]{1,0:T(8,128)S(1)}, f32[1,1]{1,0:T(1,128)S(1)}, f32[1,768]{1,0:T(1,128)S(1)}) custom-call(f32[128,768]{1,0:T(8,128)} %bitcast.10, f32[3,1,3072]{2,1,0:T(1,128)} %bitcast.11, bf16[3,3072,384]{2,1,0:T(8,128)(2,1)} %bitcast.9, f32[2,128]{1,0:T(2,128)} %gain_hbm.1, bf16[384,3072]{1,0:T(8,128)(2,1)} %wo_hbm.1, ...), custom_call_target="tpu_custom_call" | custom-call | tf_op jit(solution)/shard_map/sweep/pallas_call | solution.py:424
  43.6 0.0 copy-done
  43.6 0.9 %bitcast_add_fusion.1 = (f32[1,128,768]{2,1,0:T(8,128)}, f32[1,128,768]{2,1,0:T(8,128)}) fusion(f32[128,768]{1,0:T(8,128)S(1)} %get-tuple-element.7, f32[768]{0:T(1024)S(1)} %reduce, f32[1,128,768]{2,1,0:T(8,128)S(1)} %copy-done, f32[128,768]{1,0:T(8,128)S(1)} %get-tuple-element.9), kind=kLoop, calls=%fused_computation.1 | loop fusion | flops 294912 | bytes 1969152 | tf_op jit(solution)/shard_map/add | solution.py:478
  (1 shorter events, 0.0 us)
Async XLA Ops:
  0.6 43.0 %copy-start = (f32[1,128,768]{2,1,0:T(8,128)S(1)}, f32[1,128,768]{2,1,0:T(8,128)}, u32[]{:S(2)}) copy-start(f32[1,128,768]{2,1,0:T(8,128)} %param.6) | copy-start | bytes 1179652

commit v8 on v7

--- a/solution.py
+++ b/solution.py
@@ -177,8 +177,8 @@
     lat_copies = []
     for r in range(1, NQ):
         there = pl.ds(pl.multiple_of(lax.rem(q + r, NQ) * rows, rows), rows)
-        lat_copies.append(cp.remote(lat.at[there, :], latp.at[q], qpeer(r)))
-        lat_copies[-1].start()
+        lat_copies.append((lat.at[there, :], latp.at[q], qpeer(r)))
+    lat_copies = [cp.several(lat.at[0 : tokens - rows, :], latp.at[0 : NQ - 1], lat_copies)]
     latp[q] = lat[pl.ds(pl.multiple_of(q * rows, rows), rows), :]
 
     def project(d, k, first=False):
@@ -280,9 +280,10 @@
                 c.wait_recv()
 
     mine = pl.ds(pl.multiple_of(q * rows, rows), rows)
-    s0_c = [cp.remote(s0p, s0.at[mine, :], qpeer(r)) for r in range(1, NQ)]
-    for c in s0_c:
-        c.start()
+    most = s0.at[0 : tokens - rows, :]
+    s0_c = [
+        cp.several(most, most, [(s0p, s0.at[mine, :], qpeer(r)) for r in range(1, NQ)])
+    ]
     s0[mine, :] = s0p[...]
 
     position = (off_ref[0] + tm).astype(jnp.float32)

time: 45.9 us -> 45.9 us (level)
  no operation moved by 1% of the time
where the time goes in v8:
time: 45.9 us; the launch traced here: 45.7 us
  Pallas kernels  42.2 us (92%)
  between operations  2.52 us (5%)
  other arithmetic  0.96 us (2%)
    pallas_call x1, Pallas kernels, body(): pl.pallas_call(kernel, out_shape=(pltpu.VMEM((tokens, cols), f32), pltpu....  42.2 us
    add x1, other arithmetic, body(): return (fresh[None] + step[None] * drift, drift, residual.reshape(1))  0.95 us

profile of v8, /device:TPU:32, one launch (start us, length us, event | category | flops | bytes accessed | tf_op | source)
XLA Modules:
  0.0 45.7 jit_solution(13665087234899436813)
XLA Ops:
  0.6 0.0 copy-start
  1.3 42.2 %sweep.1 = (f32[128,768]{1,0:T(8,128)S(1)}, f32[128,768]{1,0:T(8,128)S(1)}, f32[1,1]{1,0:T(1,128)S(1)}, f32[1,768]{1,0:T(1,128)S(1)}) custom-call(f32[128,768]{1,0:T(8,128)} %bitcast.10, f32[3,1,3072]{2,1,0:T(1,128)} %bitcast.11, bf16[3,3072,384]{2,1,0:T(8,128)(2,1)} %bitcast.9, f32[2,128]{1,0:T(2,128)} %gain_hbm.1, bf16[384,3072]{1,0:T(8,128)(2,1)} %wo_hbm.1, ...), custom_call_target="tpu_custom_call" | custom-call | tf_op jit(solution)/shard_map/sweep/pallas_call | solution.py:425
  43.6 0.0 copy-done
  43.6 0.9 %bitcast_add_fusion.1 = (f32[1,128,768]{2,1,0:T(8,128)}, f32[1,128,768]{2,1,0:T(8,128)}) fusion(f32[128,768]{1,0:T(8,128)S(1)} %get-tuple-element.7, f32[768]{0:T(1024)S(1)} %reduce, f32[1,128,768]{2,1,0:T(8,128)S(1)} %copy-done, f32[128,768]{1,0:T(8,128)S(1)} %get-tuple-element.9), kind=kLoop, calls=%fused_computation.1 | loop fusion | flops 294912 | bytes 1969152 | tf_op jit(solution)/shard_map/add | solution.py:479
  (1 shorter events, 0.0 us)
Async XLA Ops:
  0.6 43.0 %copy-start = (f32[1,128,768]{2,1,0:T(8,128)S(1)}, f32[1,128,768]{2,1,0:T(8,128)}, u32[]{:S(2)}) copy-start(f32[1,128,768]{2,1,0:T(8,128)} %param.6) | copy-start | bytes 1179652
